TPU v7x, 32 devices: a whole 2x2x4 slice. The times are simulated.
32 devices in a mesh: row: 4 (over z), col: 2 (over x), rep: 4 (over y, core).
Axes of the slice: x: 2, y: 2, z: 4, core: 2. Of those that a mesh axis runs over, the one named last changes fastest.
Arguments:
- tensor_tiles: bfloat16 [64, 4, 128, 128], P(('row', 'col', 'rep')), may hold values from -12 to 12
- tile_pairs: int32 [64], P(('row', 'col', 'rep')), may hold values from 0 to 1, as said below
- tile_counts: int32 [32], P(('row', 'col', 'rep')), may hold values from 1 to 2, as said below
- occupied: bfloat16 [1024, 1024], P(('col', 'rep'), 'row'), as said below
- virtual: bfloat16 [1024, 1024], P(('col', 'rep'), 'row'), as said below
Outputs:
- polar: float32 [4, 4], replicated
- dressed: bfloat16 [1024, 4, 1024], P(('col', 'rep'), None, 'row')
Inputs may be any that keep to these rules, and one draw needn't show every extreme that they name: `tile_pairs`: the 2 entries of one block are distinct: a permutation of its tile pairs. `tile_counts`: some block has all 2 entries live. `occupied`: Symmetric. `virtual`: Symmetric.
All inputs are finite; a program needn't handle non-finite values.
Results may differ from a plain program's by a relative error of at most 0.0049.
Values may be sent and summed in bfloat16 or wider, within the bound.
No kernel may reach another device: no remote copies, remote signals or barrier semaphores. Data moves between devices by JAX's collectives and lax.ppermute only.
A program may use at most 128 MiB of HBM per device.

v0:
```python
import functools

import jax
import jax.numpy as jnp
from jax import lax
from jax.experimental import pallas as pl
from jax.experimental.pallas import tpu as pltpu
from jax.sharding import PartitionSpec as P

PLANE = ("col", "rep")
EVERY = ("row", "col", "rep")
VMEM = pl.BlockSpec(memory_space=pltpu.VMEM)
SMEM = pl.BlockSpec(memory_space=pltpu.SMEM)
ROOM = 48 << 20


def flip(value, axes, mask, count):
    return lax.ppermute(value, axes, [(i, i ^ mask) for i in range(count)])


def after(value, earlier):
    return lax.optimization_barrier((value, earlier))


def gather_row(value, n_row):
    found = {0: value}
    step = n_row // 2
    while step:
        found.update({k ^ step: flip(held, "row", step, n_row) for k, held in list(found.items())})
        step //= 2
    return [found[k] for k in range(n_row)]


def plane_index():
    return lax.axis_index("col") * lax.axis_size("rep") + lax.axis_index("rep")


def place_kernel(nu_tiles, counts_ref, pairs_any, tiles_any, weight_any, column_any, *refs):
    line_ref, bundle_ref, pairs_ref, tiles_ref, sems = refs
    slots, aux, tile, _ = tiles_ref.shape
    cut = line_ref.shape[0] - 1
    copies = [
        pltpu.make_async_copy(source, target, sems.at[i])
        for i, (source, target) in enumerate(
            [
                (tiles_any, tiles_ref),
                (pairs_any, pairs_ref),
                (weight_any, line_ref.at[cut]),
                (column_any, bundle_ref.at[aux - cut]),
            ]
        )
    ]
    for copy in copies:
        copy.start()
    for copy in copies:
        copy.wait()
    for t in range(slots):
        pair = pairs_ref[t]
        rows = pl.ds(pl.multiple_of(pair // nu_tiles * tile, tile), tile)
        cols = pl.ds(pl.multiple_of(pair % nu_tiles * tile, tile), tile)

        @pl.when(t < counts_ref[0])
        def _():
            line_ref[:cut, rows, cols] = tiles_ref[t, :cut]
            bundle_ref[: aux - cut, rows, cols] = tiles_ref[t, cut:]

        @pl.when(t >= counts_ref[0])
        def _():
            line_ref[:cut, rows, cols] = jnp.zeros((cut, tile, tile), line_ref.dtype)
            bundle_ref[: aux - cut, rows, cols] = jnp.zeros((aux - cut, tile, tile), line_ref.dtype)


def place(tile_pairs, tile_counts, tensor_tiles, weight, column):
    slots, aux, tile, _ = tensor_tiles.shape
    mu, nu = weight.shape
    cut = aux // 2
    stays = [
        pltpu.with_memory_space_constraint(value, pltpu.HBM) for value in (tile_pairs, tensor_tiles, weight, column)
    ]
    return pl.pallas_call(
        functools.partial(place_kernel, nu // tile),
        out_shape=[jax.ShapeDtypeStruct((count + 1, mu, nu), weight.dtype) for count in (cut, aux - cut)],
        in_specs=[SMEM] + [pl.BlockSpec(memory_space=pltpu.HBM)] * 4,
        out_specs=[VMEM, VMEM],
        scratch_shapes=[
            pltpu.SMEM(tile_pairs.shape, tile_pairs.dtype),
            pltpu.VMEM(tensor_tiles.shape, tensor_tiles.dtype),
            pltpu.SemaphoreType.DMA((4,)),
        ],
        compiler_params=pltpu.CompilerParams(vmem_limit_bytes=ROOM),
        cost_estimate=pl.CostEstimate(flops=0, bytes_accessed=6 * tensor_tiles.size, transcendentals=0),
        name="place",
    )(tile_counts, *stays)


def dot(left, right):
    return jnp.dot(left, right, preferred_element_type=jnp.float32)


def mix_kernel(n_row, n_plane, *refs):
    lines, bundles = refs[:n_row], refs[n_row : n_row + n_plane]
    half_ref, mixed_ref, weight_ref, panel_ref = refs[n_row + n_plane :]
    planes, mu, nu = lines[0].shape
    cut, rest = planes - 1, bundles[0].shape[0] - 1
    row, plane = lax.axis_index("row"), plane_index()
    for k in range(n_plane):
        panel_ref[pl.ds(pl.multiple_of((plane ^ k) * mu, mu), mu), :] = bundles[k][rest]
    for k in range(n_row):
        weight_ref[:, pl.ds(pl.multiple_of((row ^ k) * nu, nu), nu)] = lines[k][cut]
    for p in range(cut):
        total = jnp.zeros((mu, nu), jnp.float32)
        for k in range(n_row):
            at = pl.multiple_of((row ^ k) * nu, nu)
            total += dot(lines[k][p], panel_ref[pl.ds(at, nu), :])
        half_ref[:, p * nu : (p + 1) * nu] = total.astype(half_ref.dtype)
    for p in range(rest):
        total = jnp.zeros((mu, nu), jnp.float32)
        for k in range(n_plane):
            at = pl.multiple_of((plane ^ k) * mu, mu)
            total += dot(weight_ref[:, pl.ds(at, mu)], bundles[k][p])
        mixed_ref[:, p * nu : (p + 1) * nu] = total.astype(mixed_ref.dtype)


def mix(lines, bundles):
    planes, mu, nu = lines[0].shape
    cut, rest = planes - 1, bundles[0].shape[0] - 1
    n_row, n_plane = len(lines), len(bundles)
    kind = lines[0].dtype
    return pl.pallas_call(
        functools.partial(mix_kernel, n_row, n_plane),
        out_shape=(
            jax.ShapeDtypeStruct((mu, cut * nu), kind),
            jax.ShapeDtypeStruct((mu, rest * nu), kind),
            jax.ShapeDtypeStruct((mu, n_row * nu), kind),
            jax.ShapeDtypeStruct((n_plane * mu, nu), kind),
        ),
        in_specs=[VMEM] * (n_row + n_plane),
        out_specs=[VMEM] * 4,
        compiler_params=pltpu.CompilerParams(vmem_limit_bytes=ROOM),
        cost_estimate=pl.CostEstimate(
            flops=2 * (cut + rest) * mu * nu * nu * n_row,
            bytes_accessed=4 * n_row * (cut + rest) * mu * nu,
            transcendentals=0,
        ),
        name="mix",
    )(*lines, *bundles)


def dress_kernel(n_row, n_plane, n_all, total_ao, weight_ref, panel_ref, line_ref, bundle_ref, *refs):
    halves, mixed = refs[:n_plane], refs[n_plane : n_plane + n_row]
    out_ref, share_ref = refs[n_plane + n_row :]
    mu, aux, nu = out_ref.shape
    cut = line_ref.shape[0] - 1
    row, plane = lax.axis_index("row"), plane_index()
    lanes = lax.broadcasted_iota(jnp.int32, share_ref.shape[1:], 1)
    share = jnp.zeros(share_ref.shape[1:], jnp.float32)
    for q in range(aux):
        total = jnp.zeros((mu, nu), jnp.float32)
        if q < cut:
            for k in range(n_plane):
                at = pl.multiple_of((plane ^ k) * mu, mu)
                total += dot(weight_ref[:, pl.ds(at, mu)], halves[k][:, q * nu : (q + 1) * nu])
        else:
            for k in range(n_row):
                at = pl.multiple_of((row ^ k) * nu, nu)
                total += dot(mixed[k][:, (q - cut) * nu : (q - cut + 1) * nu], panel_ref[pl.ds(at, nu), :])
        rounded = total.astype(out_ref.dtype)
        out_ref[:, q, :] = rounded
        wide = rounded.astype(jnp.float32) if q < cut else total
        for p in range(aux):
            block = line_ref[p] if p < cut else bundle_ref[p - cut]
            folded = jnp.sum((block.astype(jnp.float32) * wide).reshape(mu // 8, 8, nu), axis=0)
            own = jnp.sum(jnp.sum(folded, axis=0, keepdims=True), axis=1, keepdims=True) / total_ao
            share = jnp.where(lanes == p * aux + q, own, share)
    for i in range(n_all):
        share_ref[i] = share


def dress(weight, panel, line, bundle, halves, mixed, n_all):
    planes, mu, nu = line.shape
    aux = planes - 1 + bundle.shape[0] - 1
    n_row, n_plane = len(mixed), len(halves)
    return pl.pallas_call(
        functools.partial(dress_kernel, n_row, n_plane, n_all, weight.shape[1]),
        out_shape=(
            jax.ShapeDtypeStruct((mu, aux, nu), line.dtype),
            jax.ShapeDtypeStruct((n_all, 1, 128), jnp.float32),
        ),
        in_specs=[VMEM] * (4 + n_plane + n_row),
        out_specs=(VMEM, VMEM),
        compiler_params=pltpu.CompilerParams(vmem_limit_bytes=ROOM),
        cost_estimate=pl.CostEstimate(
            flops=2 * aux * mu * mu * nu * n_plane, bytes_accessed=4 * n_plane * aux * mu * nu, transcendentals=0
        ),
        name="dress",
    )(weight, panel, line, bundle, *halves, *mixed)


def finish_kernel(shares_ref, out_ref):
    aux = out_ref.shape[0]
    polar = jnp.sum(shares_ref[...], axis=0)
    for p in range(aux):
        out_ref[p : p + 1, :] = polar[:, p * aux : (p + 1) * aux]


def finish(shares, aux):
    return pl.pallas_call(
        finish_kernel,
        out_shape=jax.ShapeDtypeStruct((aux, aux), jnp.float32),
        in_specs=[VMEM],
        out_specs=VMEM,
        compiler_params=pltpu.CompilerParams(vmem_limit_bytes=ROOM),
        name="finish",
    )(shares)


def on_device(tensor_tiles, tile_pairs, tile_counts, occupied, virtual):
    aux = tensor_tiles.shape[1]
    n_row, n_plane = lax.axis_size("row"), lax.axis_size("col") * lax.axis_size("rep")
    near = list(range(2, n_plane, 2))
    sibling = lambda value: flip(value, PLANE, 1, n_plane)

    def gather_plane(value):
        values = [value] + [flip(value, PLANE, k, n_plane) for k in near]
        return [held for value in values for held in (value, sibling(value))]

    line, bundle = place(tile_pairs, tile_counts, tensor_tiles, occupied, virtual)
    half, mixed, weight, panel = mix(gather_row(line, n_row), gather_plane(bundle))
    halves, mixed = gather_plane(half), gather_row(mixed, n_row)
    dressed, shares = dress(weight, panel, line, bundle, halves, mixed, n_row * n_plane)
    polar = finish(lax.all_to_all(shares, EVERY, 0, 0), aux)
    return polar, dressed


def solution(mesh):
    return jax.shard_map(
        on_device,
        mesh=mesh,
        in_specs=(P(EVERY, None, None, None), P(EVERY), P(EVERY), P(PLANE, "row"), P(PLANE, "row")),
        out_specs=(P(), P(PLANE, None, "row")),
        check_vma=False,
    )
```

profile of v0, /device:TPU:0, one launch (start us, length us, event | category | flops | bytes accessed | tf_op | source)
XLA Modules:
  0.0 53.4 jit_solution(1720487259316389083)
XLA Ops:
  1.3 1.1 %place.1 = (bf16[3,128,256]{2,1,0:T(8,128)(2,1)S(1)}, bf16[3,128,256]{2,1,0:T(8,128)(2,1)S(1)}) custom-call(s32[1]{0:T(128)S(6)} %copy.7.counts_ref, s32[2]{0:T(128)} %pairs_any.1, bf16[2,4,128,128]{3,2,1,0:T(8,128)(2,1)} %tiles_any.1, bf16[128,256]{1,0:T(8,128)(2,1)} %weight_any.1, bf16[128,256]{1,0:T(8,128)(2,1)} %column_any.1), custom_call_target="tpu_custom_call" | custom-call | bytes 786432 | tf_op jit(solution)/shard_map/place/pallas_call | solution.py:80
  2.4 4.1 %collective-permute-start.1 = (bf16[3,128,256]{2,1,0:T(8,128)(2,1)S(1)}, bf16[3,128,256]{2,1,0:T(8,128)(2,1)S(1)}, u32[]{:S(2)}, u32[]{:S(2)}) collective-permute-start(bf16[3,128,256]{2,1,0:T(8,128)(2,1)S(1)} %get-tuple-element.10.refs_0_.line_ref), channel_id=1, source_target_pairs={{0,16},{8,24},{16,0},{24,8},{1,17},{9,25},{17,1},{25,9},{2,18},{10... | collective-permute-start | bytes 589832 | tf_op jit(solution)/shard_map/ppermute | solution.py:18
  6.5 1.6 %collective-permute-start = (bf16[3,128,256]{2,1,0:T(8,128)(2,1)S(1)}, bf16[3,128,256]{2,1,0:T(8,128)(2,1)S(1)}, u32[]{:S(2)}, u32[]{:S(2)}) collective-permute-start(bf16[3,128,256]{2,1,0:T(8,128)(2,1)S(1)} %get-tuple-element.10.refs_0_.line_ref), channel_id=1, source_target_pairs={{0,8},{8,0},{16,24},{24,16},{1,9},{9,1},{17,25},{25,17},{2,10},{10... | collective-permute-start | bytes 589832 | tf_op jit(solution)/shard_map/ppermute | solution.py:18
  8.0 2.4 %collective-permute-start.8 = (bf16[3,128,256]{2,1,0:T(8,128)(2,1)S(1)}, bf16[3,128,256]{2,1,0:T(8,128)(2,1)S(1)}, u32[]{:S(2)}, u32[]{:S(2)}) collective-permute-start(bf16[3,128,256]{2,1,0:T(8,128)(2,1)S(1)} %get-tuple-element.11.refs_4_.bundle_ref), channel_id=1, source_target_pairs={{0,6},{1,7},{2,4},{3,5},{4,2},{5,3},{6,0},{7,1},{8,14},{9,15},{10,... | collective-permute-start | bytes 589832 | tf_op jit(solution)/shard_map/ppermute | solution.py:18
  10.5 0.5 %collective-permute-start.6 = (bf16[3,128,256]{2,1,0:T(8,128)(2,1)S(1)}, bf16[3,128,256]{2,1,0:T(8,128)(2,1)S(1)}, u32[]{:S(2)}, u32[]{:S(2)}) collective-permute-start(bf16[3,128,256]{2,1,0:T(8,128)(2,1)S(1)} %get-tuple-element.11.refs_4_.bundle_ref), channel_id=1, source_target_pairs={{0,4},{1,5},{2,6},{3,7},{4,0},{5,1},{6,2},{7,3},{8,12},{9,13},{10,... | collective-permute-start | bytes 589832 | tf_op jit(solution)/shard_map/ppermute | solution.py:18
  11.0 0.5 collective-permute-start.4
  11.5 4.2 %collective-permute-done.1.refs_2_ = bf16[3,128,256]{2,1,0:T(8,128)(2,1)S(1)} collective-permute-done((bf16[3,128,256]{2,1,0:T(8,128)(2,1)S(1)}, bf16[3,128,256]{2,1,0:T(8,128)(2,1)S(1)}, u32[]{:S(2)}, u32[]{:S(2)}) %collective-permute-start.1) | collective-permute-done | bytes 196640 | tf_op jit(solution)/shard_map/ppermute | solution.py:18
  15.9 1.5 %collective-permute-start.2 = (bf16[3,128,256]{2,1,0:T(8,128)(2,1)S(1)}, bf16[3,128,256]{2,1,0:T(8,128)(2,1)S(1)}, u32[]{:S(2)}, u32[]{:S(2)}) collective-permute-start(bf16[3,128,256]{2,1,0:T(8,128)(2,1)S(1)} %collective-permute-done.1.refs_2_), channel_id=1, source_target_pairs={{0,8},{8,0},{16,24},{24,16},{1,9},{9,1},{17,25},{25,17},{2,10},{10... | collective-permute-start | bytes 589832 | tf_op jit(solution)/shard_map/ppermute | solution.py:18
  17.4 2.0 %collective-permute-done.6.refs_8_ = bf16[3,128,256]{2,1,0:T(8,128)(2,1)S(1)} collective-permute-done((bf16[3,128,256]{2,1,0:T(8,128)(2,1)S(1)}, bf16[3,128,256]{2,1,0:T(8,128)(2,1)S(1)}, u32[]{:S(2)}, u32[]{:S(2)}) %collective-permute-start.6) | collective-permute-done | bytes 196640 | tf_op jit(solution)/shard_map/ppermute | solution.py:18
  19.8 3.2 %collective-permute-done.2.refs_3_ = bf16[3,128,256]{2,1,0:T(8,128)(2,1)S(1)} collective-permute-done((bf16[3,128,256]{2,1,0:T(8,128)(2,1)S(1)}, bf16[3,128,256]{2,1,0:T(8,128)(2,1)S(1)}, u32[]{:S(2)}, u32[]{:S(2)}) %collective-permute-start.2) | collective-permute-done | bytes 196640 | tf_op jit(solution)/shard_map/ppermute | solution.py:18
  23.0 0.6 %mix.1 = (bf16[128,512]{1,0:T(8,128)(2,1)S(1)}, bf16[128,512]{1,0:T(8,128)(2,1)S(1)}, bf16[128,1024]{1,0:T(8,128)(2,1)S(1)}, bf16[1024,256]{1,0:T(8,128)(2,1)S(1)}) custom-call(bf16[3,128,256]{2,1,0:T(8,128)(2,1)S(1)} %get-tuple-element.10.refs_0_.line_ref, bf16[3,128,256]{2,1,0:T(8,128)(2,1)S(1)} %collective-permute-done.refs_1_, ...), custom_call_target="tpu_custom_call" | custom-call | flops 268435456 | bytes 2097152 | tf_op jit(solution)/shard_map/mix/pallas_call | solution.py:129
  23.7 2.3 %collective-permute-start.18 = (bf16[128,512]{1,0:T(8,128)(2,1)S(1)}, bf16[128,512]{1,0:T(8,128)(2,1)S(1)}, u32[]{:S(2)}, u32[]{:S(2)}) collective-permute-start(bf16[128,512]{1,0:T(8,128)(2,1)S(1)} %get-tuple-element.15.refs_8_), channel_id=1, source_target_pairs={{0,16},{8,24},{16,0},{24,8},{1,17},{9,25},{17,1},{25,9},{2,18},{10... | collective-permute-start | bytes 393224 | tf_op jit(solution)/shard_map/ppermute | solution.py:18
  26.0 1.7 %collective-permute-start.17 = (bf16[128,512]{1,0:T(8,128)(2,1)S(1)}, bf16[128,512]{1,0:T(8,128)(2,1)S(1)}, u32[]{:S(2)}, u32[]{:S(2)}) collective-permute-start(bf16[128,512]{1,0:T(8,128)(2,1)S(1)} %get-tuple-element.15.refs_8_), channel_id=1, source_target_pairs={{0,8},{8,0},{16,24},{24,16},{1,9},{9,1},{17,25},{25,17},{2,10},{10... | collective-permute-start | bytes 393224 | tf_op jit(solution)/shard_map/ppermute | solution.py:18
  27.7 2.4 %collective-permute-start.15 = (bf16[128,512]{1,0:T(8,128)(2,1)S(1)}, bf16[128,512]{1,0:T(8,128)(2,1)S(1)}, u32[]{:S(2)}, u32[]{:S(2)}) collective-permute-start(bf16[128,512]{1,0:T(8,128)(2,1)S(1)} %get-tuple-element.14.refs_0_), channel_id=1, source_target_pairs={{0,6},{1,7},{2,4},{3,5},{4,2},{5,3},{6,0},{7,1},{8,14},{9,15},{10,... | collective-permute-start | bytes 393224 | tf_op jit(solution)/shard_map/ppermute | solution.py:18
  30.2 0.5 %collective-permute-start.13 = (bf16[128,512]{1,0:T(8,128)(2,1)S(1)}, bf16[128,512]{1,0:T(8,128)(2,1)S(1)}, u32[]{:S(2)}, u32[]{:S(2)}) collective-permute-start(bf16[128,512]{1,0:T(8,128)(2,1)S(1)} %get-tuple-element.14.refs_0_), channel_id=1, source_target_pairs={{0,4},{1,5},{2,6},{3,7},{4,0},{5,1},{6,2},{7,3},{8,12},{9,13},{10,... | collective-permute-start | bytes 393224 | tf_op jit(solution)/shard_map/ppermute | solution.py:18
  30.7 0.5 collective-permute-start.11
  31.2 1.3 %collective-permute-done.18.refs_10_ = bf16[128,512]{1,0:T(8,128)(2,1)S(1)} collective-permute-done((bf16[128,512]{1,0:T(8,128)(2,1)S(1)}, bf16[128,512]{1,0:T(8,128)(2,1)S(1)}, u32[]{:S(2)}, u32[]{:S(2)}) %collective-permute-start.18) | collective-permute-done | bytes 131104 | tf_op jit(solution)/shard_map/ppermute | solution.py:18
  32.8 1.4 %collective-permute-start.19 = (bf16[128,512]{1,0:T(8,128)(2,1)S(1)}, bf16[128,512]{1,0:T(8,128)(2,1)S(1)}, u32[]{:S(2)}, u32[]{:S(2)}) collective-permute-start(bf16[128,512]{1,0:T(8,128)(2,1)S(1)} %collective-permute-done.18.refs_10_), channel_id=1, source_target_pairs={{0,8},{8,0},{16,24},{24,16},{1,9},{9,1},{17,25},{25,17},{2,10},{10... | collective-permute-start | bytes 393224 | tf_op jit(solution)/shard_map/ppermute | solution.py:18
  34.1 0.6 %collective-permute-done.15.refs_6_ = bf16[128,512]{1,0:T(8,128)(2,1)S(1)} collective-permute-done((bf16[128,512]{1,0:T(8,128)(2,1)S(1)}, bf16[128,512]{1,0:T(8,128)(2,1)S(1)}, u32[]{:S(2)}, u32[]{:S(2)}) %collective-permute-start.15) | collective-permute-done | bytes 131104 | tf_op jit(solution)/shard_map/ppermute | solution.py:18
  34.7 1.3 %collective-permute-done.13.refs_4_ = bf16[128,512]{1,0:T(8,128)(2,1)S(1)} collective-permute-done((bf16[128,512]{1,0:T(8,128)(2,1)S(1)}, bf16[128,512]{1,0:T(8,128)(2,1)S(1)}, u32[]{:S(2)}, u32[]{:S(2)}) %collective-permute-start.13) | collective-permute-done | bytes 131104 | tf_op jit(solution)/shard_map/ppermute | solution.py:18
  36.6 1.8 %collective-permute-done.19.refs_11_ = bf16[128,512]{1,0:T(8,128)(2,1)S(1)} collective-permute-done((bf16[128,512]{1,0:T(8,128)(2,1)S(1)}, bf16[128,512]{1,0:T(8,128)(2,1)S(1)}, u32[]{:S(2)}, u32[]{:S(2)}) %collective-permute-start.19) | collective-permute-done | bytes 131104 | tf_op jit(solution)/shard_map/ppermute | solution.py:18
  38.4 1.7 %dress.1 = (bf16[128,4,256]{2,1,0:T(4,128)(2,1)}, f32[32,1,128]{2,1,0:T(1,128)S(1)}) custom-call(bf16[128,1024]{1,0:T(8,128)(2,1)S(1)} %get-tuple-element.12.weight_ref, bf16[1024,256]{1,0:T(8,128)(2,1)S(1)} %get-tuple-element.13.panel_ref, bf16[3,128,256]{2,1,0:T(8,128)(2,1)S(1)} %get-tuple-element.10.refs_0_.line_ref, ...), custom_call_target="tpu_custom_call" | custom-call | flops 268435456 | bytes 4194304 | tf_op jit(solution)/shard_map/dress/pallas_call | solution.py:183
  40.1 12.6 %all_to_all.5.shares_ref = f32[32,1,128]{2,1,0:T(1,128)S(1)} all-to-all(f32[32,1,128]{2,1,0:T(1,128)S(1)} %get-tuple-element.16), channel_id=1, replica_groups=mesh['row'=4,'col'=2,'rep'=4] {'row','col','rep'}, dimensions={0} | all-to-all | bytes 32768 | tf_op jit(solution)/shard_map/all_to_all | solution.py:231
  52.7 0.7 %finish.1 = f32[4,4]{1,0:T(4,128)} custom-call(f32[32,1,128]{2,1,0:T(1,128)S(1)} %all_to_all.5.shares_ref), custom_call_target="tpu_custom_call" | custom-call | tf_op jit(solution)/shard_map/finish/pallas_call | solution.py:207
  (21 shorter events, 1.5 us)
Async XLA Ops:
  2.4 13.3 %collective-permute-start.1 = (bf16[3,128,256]{2,1,0:T(8,128)(2,1)S(1)}, bf16[3,128,256]{2,1,0:T(8,128)(2,1)S(1)}, u32[]{:S(2)}, u32[]{:S(2)}) collective-permute-start(bf16[3,128,256]{2,1,0:T(8,128)(2,1)S(1)} %get-tuple-element.10.refs_0_.line_ref), channel_id=1, source_target_pairs={{0,16},{8,24},{16,0},{24,8},{1,17},{9,25},{17,1},{25,9},{2,18},{10... | collective-permute-start | bytes 589832 | tf_op jit(solution)/shard_map/ppermute | solution.py:18
  6.5 9.4 %collective-permute-start = (bf16[3,128,256]{2,1,0:T(8,128)(2,1)S(1)}, bf16[3,128,256]{2,1,0:T(8,128)(2,1)S(1)}, u32[]{:S(2)}, u32[]{:S(2)}) collective-permute-start(bf16[3,128,256]{2,1,0:T(8,128)(2,1)S(1)} %get-tuple-element.10.refs_0_.line_ref), channel_id=1, source_target_pairs={{0,8},{8,0},{16,24},{24,16},{1,9},{9,1},{17,25},{25,17},{2,10},{10... | collective-permute-start | bytes 589832 | tf_op jit(solution)/shard_map/ppermute | solution.py:18
  8.0 9.3 %collective-permute-start.8 = (bf16[3,128,256]{2,1,0:T(8,128)(2,1)S(1)}, bf16[3,128,256]{2,1,0:T(8,128)(2,1)S(1)}, u32[]{:S(2)}, u32[]{:S(2)}) collective-permute-start(bf16[3,128,256]{2,1,0:T(8,128)(2,1)S(1)} %get-tuple-element.11.refs_4_.bundle_ref), channel_id=1, source_target_pairs={{0,6},{1,7},{2,4},{3,5},{4,2},{5,3},{6,0},{7,1},{8,14},{9,15},{10,... | collective-permute-start | bytes 589832 | tf_op jit(solution)/shard_map/ppermute | solution.py:18
  10.5 8.8 %collective-permute-start.6 = (bf16[3,128,256]{2,1,0:T(8,128)(2,1)S(1)}, bf16[3,128,256]{2,1,0:T(8,128)(2,1)S(1)}, u32[]{:S(2)}, u32[]{:S(2)}) collective-permute-start(bf16[3,128,256]{2,1,0:T(8,128)(2,1)S(1)} %get-tuple-element.11.refs_4_.bundle_ref), channel_id=1, source_target_pairs={{0,4},{1,5},{2,6},{3,7},{4,0},{5,1},{6,2},{7,3},{8,12},{9,13},{10,... | collective-permute-start | bytes 589832 | tf_op jit(solution)/shard_map/ppermute | solution.py:18
  11.0 8.3 %collective-permute-start.4 = (bf16[3,128,256]{2,1,0:T(8,128)(2,1)S(1)}, bf16[3,128,256]{2,1,0:T(8,128)(2,1)S(1)}, u32[]{:S(2)}, u32[]{:S(2)}) collective-permute-start(bf16[3,128,256]{2,1,0:T(8,128)(2,1)S(1)} %get-tuple-element.11.refs_4_.bundle_ref), channel_id=1, source_target_pairs={{0,2},{1,3},{2,0},{3,1},{4,6},{5,7},{6,4},{7,5},{8,10},{9,11},{10,... | collective-permute-start | bytes 589832 | tf_op jit(solution)/shard_map/ppermute | solution.py:18
  15.7 4.2 %collective-permute-start.3 = (bf16[3,128,256]{2,1,0:T(8,128)(2,1)S(1)}, bf16[3,128,256]{2,1,0:T(8,128)(2,1)S(1)}, u32[]{:S(2)}, u32[]{:S(2)}) collective-permute-start(bf16[3,128,256]{2,1,0:T(8,128)(2,1)S(1)} %get-tuple-element.11.refs_4_.bundle_ref), channel_id=1, source_target_pairs={{0,1},{1,0},{2,3},{3,2},{4,5},{5,4},{6,7},{7,6},{8,9},{9,8},{10,11... | collective-permute-start | bytes 589832 | tf_op jit(solution)/shard_map/ppermute | solution.py:18
  15.9 7.1 %collective-permute-start.2 = (bf16[3,128,256]{2,1,0:T(8,128)(2,1)S(1)}, bf16[3,128,256]{2,1,0:T(8,128)(2,1)S(1)}, u32[]{:S(2)}, u32[]{:S(2)}) collective-permute-start(bf16[3,128,256]{2,1,0:T(8,128)(2,1)S(1)} %collective-permute-done.1.refs_2_), channel_id=1, source_target_pairs={{0,8},{8,0},{16,24},{24,16},{1,9},{9,1},{17,25},{25,17},{2,10},{10... | collective-permute-start | bytes 589832 | tf_op jit(solution)/shard_map/ppermute | solution.py:18
  17.4 5.6 %collective-permute-start.9 = (bf16[3,128,256]{2,1,0:T(8,128)(2,1)S(1)}, bf16[3,128,256]{2,1,0:T(8,128)(2,1)S(1)}, u32[]{:S(2)}, u32[]{:S(2)}) collective-permute-start(bf16[3,128,256]{2,1,0:T(8,128)(2,1)S(1)} %collective-permute-done.8.refs_10_), channel_id=1, source_target_pairs={{0,1},{1,0},{2,3},{3,2},{4,5},{5,4},{6,7},{7,6},{8,9},{9,8},{10,11... | collective-permute-start | bytes 589832 | tf_op jit(solution)/shard_map/ppermute | solution.py:18
  19.3 3.7 %collective-permute-start.7 = (bf16[3,128,256]{2,1,0:T(8,128)(2,1)S(1)}, bf16[3,128,256]{2,1,0:T(8,128)(2,1)S(1)}, u32[]{:S(2)}, u32[]{:S(2)}) collective-permute-start(bf16[3,128,256]{2,1,0:T(8,128)(2,1)S(1)} %collective-permute-done.6.refs_8_), channel_id=1, source_target_pairs={{0,1},{1,0},{2,3},{3,2},{4,5},{5,4},{6,7},{7,6},{8,9},{9,8},{10,11... | collective-permute-start | bytes 589832 | tf_op jit(solution)/shard_map/ppermute | solution.py:18
  19.3 3.7 %collective-permute-start.5 = (bf16[3,128,256]{2,1,0:T(8,128)(2,1)S(1)}, bf16[3,128,256]{2,1,0:T(8,128)(2,1)S(1)}, u32[]{:S(2)}, u32[]{:S(2)}) collective-permute-start(bf16[3,128,256]{2,1,0:T(8,128)(2,1)S(1)} %collective-permute-done.4.refs_6_), channel_id=1, source_target_pairs={{0,1},{1,0},{2,3},{3,2},{4,5},{5,4},{6,7},{7,6},{8,9},{9,8},{10,11... | collective-permute-start | bytes 589832 | tf_op jit(solution)/shard_map/ppermute | solution.py:18
  23.7 8.8 %collective-permute-start.18 = (bf16[128,512]{1,0:T(8,128)(2,1)S(1)}, bf16[128,512]{1,0:T(8,128)(2,1)S(1)}, u32[]{:S(2)}, u32[]{:S(2)}) collective-permute-start(bf16[128,512]{1,0:T(8,128)(2,1)S(1)} %get-tuple-element.15.refs_8_), channel_id=1, source_target_pairs={{0,16},{8,24},{16,0},{24,8},{1,17},{9,25},{17,1},{25,9},{2,18},{10... | collective-permute-start | bytes 393224 | tf_op jit(solution)/shard_map/ppermute | solution.py:18
  26.0 6.8 %collective-permute-start.17 = (bf16[128,512]{1,0:T(8,128)(2,1)S(1)}, bf16[128,512]{1,0:T(8,128)(2,1)S(1)}, u32[]{:S(2)}, u32[]{:S(2)}) collective-permute-start(bf16[128,512]{1,0:T(8,128)(2,1)S(1)} %get-tuple-element.15.refs_8_), channel_id=1, source_target_pairs={{0,8},{8,0},{16,24},{24,16},{1,9},{9,1},{17,25},{25,17},{2,10},{10... | collective-permute-start | bytes 393224 | tf_op jit(solution)/shard_map/ppermute | solution.py:18
  27.7 7.0 %collective-permute-start.15 = (bf16[128,512]{1,0:T(8,128)(2,1)S(1)}, bf16[128,512]{1,0:T(8,128)(2,1)S(1)}, u32[]{:S(2)}, u32[]{:S(2)}) collective-permute-start(bf16[128,512]{1,0:T(8,128)(2,1)S(1)} %get-tuple-element.14.refs_0_), channel_id=1, source_target_pairs={{0,6},{1,7},{2,4},{3,5},{4,2},{5,3},{6,0},{7,1},{8,14},{9,15},{10,... | collective-permute-start | bytes 393224 | tf_op jit(solution)/shard_map/ppermute | solution.py:18
  30.2 5.9 %collective-permute-start.13 = (bf16[128,512]{1,0:T(8,128)(2,1)S(1)}, bf16[128,512]{1,0:T(8,128)(2,1)S(1)}, u32[]{:S(2)}, u32[]{:S(2)}) collective-permute-start(bf16[128,512]{1,0:T(8,128)(2,1)S(1)} %get-tuple-element.14.refs_0_), channel_id=1, source_target_pairs={{0,4},{1,5},{2,6},{3,7},{4,0},{5,1},{6,2},{7,3},{8,12},{9,13},{10,... | collective-permute-start | bytes 393224 | tf_op jit(solution)/shard_map/ppermute | solution.py:18
  30.7 5.4 %collective-permute-start.11 = (bf16[128,512]{1,0:T(8,128)(2,1)S(1)}, bf16[128,512]{1,0:T(8,128)(2,1)S(1)}, u32[]{:S(2)}, u32[]{:S(2)}) collective-permute-start(bf16[128,512]{1,0:T(8,128)(2,1)S(1)} %get-tuple-element.14.refs_0_), channel_id=1, source_target_pairs={{0,2},{1,3},{2,0},{3,1},{4,6},{5,7},{6,4},{7,5},{8,10},{9,11},{10,... | collective-permute-start | bytes 393224 | tf_op jit(solution)/shard_map/ppermute | solution.py:18
  32.5 4.1 %collective-permute-start.10 = (bf16[128,512]{1,0:T(8,128)(2,1)S(1)}, bf16[128,512]{1,0:T(8,128)(2,1)S(1)}, u32[]{:S(2)}, u32[]{:S(2)}) collective-permute-start(bf16[128,512]{1,0:T(8,128)(2,1)S(1)} %get-tuple-element.14.refs_0_), channel_id=1, source_target_pairs={{0,1},{1,0},{2,3},{3,2},{4,5},{5,4},{6,7},{7,6},{8,9},{9,8},{10,11... | collective-permute-start | bytes 393224 | tf_op jit(solution)/shard_map/ppermute | solution.py:18
  32.8 5.6 %collective-permute-start.19 = (bf16[128,512]{1,0:T(8,128)(2,1)S(1)}, bf16[128,512]{1,0:T(8,128)(2,1)S(1)}, u32[]{:S(2)}, u32[]{:S(2)}) collective-permute-start(bf16[128,512]{1,0:T(8,128)(2,1)S(1)} %collective-permute-done.18.refs_10_), channel_id=1, source_target_pairs={{0,8},{8,0},{16,24},{24,16},{1,9},{9,1},{17,25},{25,17},{2,10},{10... | collective-permute-start | bytes 393224 | tf_op jit(solution)/shard_map/ppermute | solution.py:18
  34.7 3.7 %collective-permute-start.16 = (bf16[128,512]{1,0:T(8,128)(2,1)S(1)}, bf16[128,512]{1,0:T(8,128)(2,1)S(1)}, u32[]{:S(2)}, u32[]{:S(2)}) collective-permute-start(bf16[128,512]{1,0:T(8,128)(2,1)S(1)} %collective-permute-done.15.refs_6_), channel_id=1, source_target_pairs={{0,1},{1,0},{2,3},{3,2},{4,5},{5,4},{6,7},{7,6},{8,9},{9,8},{10,11... | collective-permute-start | bytes 393224 | tf_op jit(solution)/shard_map/ppermute | solution.py:18
  36.0 2.4 %collective-permute-start.14 = (bf16[128,512]{1,0:T(8,128)(2,1)S(1)}, bf16[128,512]{1,0:T(8,128)(2,1)S(1)}, u32[]{:S(2)}, u32[]{:S(2)}) collective-permute-start(bf16[128,512]{1,0:T(8,128)(2,1)S(1)} %collective-permute-done.13.refs_4_), channel_id=1, source_target_pairs={{0,1},{1,0},{2,3},{3,2},{4,5},{5,4},{6,7},{7,6},{8,9},{9,8},{10,11... | collective-permute-start | bytes 393224 | tf_op jit(solution)/shard_map/ppermute | solution.py:18
  36.1 2.3 %collective-permute-start.12 = (bf16[128,512]{1,0:T(8,128)(2,1)S(1)}, bf16[128,512]{1,0:T(8,128)(2,1)S(1)}, u32[]{:S(2)}, u32[]{:S(2)}) collective-permute-start(bf16[128,512]{1,0:T(8,128)(2,1)S(1)} %collective-permute-done.11.refs_2_), channel_id=1, source_target_pairs={{0,1},{1,0},{2,3},{3,2},{4,5},{5,4},{6,7},{7,6},{8,9},{9,8},{10,11... | collective-permute-start | bytes 393224 | tf_op jit(solution)/shard_map/ppermute | solution.py:18
where the time goes:
time: 53.5 us; the launch traced here: 53.4 us
  starting transfers between devices  20.5 us (38%)
  waiting for transfers between devices  14.8 us (28%)
  blocking collectives  12.6 us (24%)
  Pallas kernels  4.06 us (8%)
  between operations  1.32 us (2%)
    ppermute x20, starting transfers between devices, flip(): return lax.ppermute(value, axes, [(i, i ^ mask) for i in range(count)])  20.5 us
    ppermute x20, waiting for transfers between devices, flip(): return lax.ppermute(value, axes, [(i, i ^ mask) for i in range(count)])  14.8 us
    all_to_all x1, blocking collectives, on_device(): polar = finish(lax.all_to_all(shares, EVERY, 0, 0), aux)  12.6 us
    pallas_call x1, Pallas kernels, dress(): pl.pallas_call(functools.partial(dress_kernel, n_row, n_plane, n_all, wei...  1.67 us
    pallas_call x1, Pallas kernels, place(): pl.pallas_call(functools.partial(place_kernel, nu // tile), out_shape=[ja...  1.08 us
  transfers between devices with their start and end apart: 20, of which 10 were waited for; matrix products, arithmetic and copies ran while one was open for 0% of the time, Pallas kernels for 0%

commit v1 on v0

--- a/solution.py
+++ b/solution.py
@@ -20,6 +20,25 @@
 
 def after(value, earlier):
     return lax.optimization_barrier((value, earlier))
+
+
+def split_kernel(value_ref, block_ref, weight_ref):
+    cut = block_ref.shape[0]
+    block_ref[...] = value_ref[:cut]
+    weight_ref[...] = value_ref[cut:]
+
+
+def split(value):
+    planes, mu, nu = value.shape
+    return pl.pallas_call(
+        split_kernel,
+        out_shape=[jax.ShapeDtypeStruct((count, mu, nu), value.dtype) for count in (planes - 1, 1)],
+        in_specs=[VMEM],
+        out_specs=[VMEM, VMEM],
+        compiler_params=pltpu.CompilerParams(vmem_limit_bytes=ROOM),
+        cost_estimate=pl.CostEstimate(flops=0, bytes_accessed=4 * value.size, transcendentals=0),
+        name="split",
+    )(value)
 
 
 def gather_row(value, n_row):
@@ -98,51 +117,72 @@
 
 
 def mix_kernel(n_row, n_plane, *refs):
+    weights, bundles = refs[:n_row], refs[n_row : n_row + n_plane]
+    mixed_ref, weight_ref = refs[n_row + n_plane :]
+    _, mu, nu = weights[0].shape
+    row, plane = lax.axis_index("row"), plane_index()
+    for k, ref in enumerate(weights):
+        weight_ref[:, pl.ds(pl.multiple_of((row ^ k) * nu, nu), nu)] = ref[ref.shape[0] - 1]
+    for p in range(bundles[0].shape[0] - 1):
+        total = jnp.zeros((mu, nu), jnp.float32)
+        for k in range(n_plane):
+            at = pl.multiple_of((plane ^ k) * mu, mu)
+            total += dot(weight_ref[:, pl.ds(at, mu)], bundles[k][p])
+        mixed_ref[:, p * nu : (p + 1) * nu] = total.astype(mixed_ref.dtype)
+
+
+def mix(weights, bundles):
+    planes, mu, nu = bundles[0].shape
+    n_row, n_plane = len(weights), len(bundles)
+    kind = weights[0].dtype
+    return pl.pallas_call(
+        functools.partial(mix_kernel, n_row, n_plane),
+        out_shape=(
+            jax.ShapeDtypeStruct((mu, (planes - 1) * nu), kind),
+            jax.ShapeDtypeStruct((mu, n_row * nu), kind),
+        ),
+        in_specs=[VMEM] * (n_row + n_plane),
+        out_specs=[VMEM] * 2,
+        compiler_params=pltpu.CompilerParams(vmem_limit_bytes=ROOM),
+        cost_estimate=pl.CostEstimate(
+            flops=2 * planes * mu * nu * nu * n_row, bytes_accessed=4 * n_row * planes * mu * nu, transcendentals=0
+        ),
+        name="mix",
+    )(*weights, *bundles)
+
+
+def half_kernel(cut, n_row, n_plane, *refs):
     lines, bundles = refs[:n_row], refs[n_row : n_row + n_plane]
-    half_ref, mixed_ref, weight_ref, panel_ref = refs[n_row + n_plane :]
-    planes, mu, nu = lines[0].shape
-    cut, rest = planes - 1, bundles[0].shape[0] - 1
+    half_ref, panel_ref = refs[n_row + n_plane :]
+    planes, mu, nu = bundles[0].shape
     row, plane = lax.axis_index("row"), plane_index()
     for k in range(n_plane):
-        panel_ref[pl.ds(pl.multiple_of((plane ^ k) * mu, mu), mu), :] = bundles[k][rest]
-    for k in range(n_row):
-        weight_ref[:, pl.ds(pl.multiple_of((row ^ k) * nu, nu), nu)] = lines[k][cut]
+        panel_ref[pl.ds(pl.multiple_of((plane ^ k) * mu, mu), mu), :] = bundles[k][planes - 1]
     for p in range(cut):
         total = jnp.zeros((mu, nu), jnp.float32)
         for k in range(n_row):
             at = pl.multiple_of((row ^ k) * nu, nu)
             total += dot(lines[k][p], panel_ref[pl.ds(at, nu), :])
         half_ref[:, p * nu : (p + 1) * nu] = total.astype(half_ref.dtype)
-    for p in range(rest):
-        total = jnp.zeros((mu, nu), jnp.float32)
-        for k in range(n_plane):
-            at = pl.multiple_of((plane ^ k) * mu, mu)
-            total += dot(weight_ref[:, pl.ds(at, mu)], bundles[k][p])
-        mixed_ref[:, p * nu : (p + 1) * nu] = total.astype(mixed_ref.dtype)
-
-
-def mix(lines, bundles):
+
+
+def half_of(lines, bundles):
     planes, mu, nu = lines[0].shape
-    cut, rest = planes - 1, bundles[0].shape[0] - 1
-    n_row, n_plane = len(lines), len(bundles)
+    cut, n_row, n_plane = planes - 1, len(lines), len(bundles)
     kind = lines[0].dtype
     return pl.pallas_call(
-        functools.partial(mix_kernel, n_row, n_plane),
+        functools.partial(half_kernel, cut, n_row, n_plane),
         out_shape=(
             jax.ShapeDtypeStruct((mu, cut * nu), kind),
-            jax.ShapeDtypeStruct((mu, rest * nu), kind),
-            jax.ShapeDtypeStruct((mu, n_row * nu), kind),
             jax.ShapeDtypeStruct((n_plane * mu, nu), kind),
         ),
         in_specs=[VMEM] * (n_row + n_plane),
-        out_specs=[VMEM] * 4,
+        out_specs=[VMEM] * 2,
         compiler_params=pltpu.CompilerParams(vmem_limit_bytes=ROOM),
         cost_estimate=pl.CostEstimate(
-            flops=2 * (cut + rest) * mu * nu * nu * n_row,
-            bytes_accessed=4 * n_row * (cut + rest) * mu * nu,
-            transcendentals=0,
-        ),
-        name="mix",
+            flops=2 * cut * mu * nu * nu * n_row, bytes_accessed=4 * n_row * cut * mu * nu, transcendentals=0
+        ),
+        name="half_product",
     )(*lines, *bundles)
 
 
@@ -221,12 +261,26 @@
     sibling = lambda value: flip(value, PLANE, 1, n_plane)
 
     def gather_plane(value):
-        values = [value] + [flip(value, PLANE, k, n_plane) for k in near]
+        return [value] + [flip(value, PLANE, k, n_plane) for k in near]
+
+    def with_siblings(values):
         return [held for value in values for held in (value, sibling(value))]
 
     line, bundle = place(tile_pairs, tile_counts, tensor_tiles, occupied, virtual)
-    half, mixed, weight, panel = mix(gather_row(line, n_row), gather_plane(bundle))
-    halves, mixed = gather_plane(half), gather_row(mixed, n_row)
+    far, step = {0: line}, n_row // 2
+    while step > 1:
+        far.update({k ^ step: flip(held, "row", step, n_row) for k, held in list(far.items())})
+        step //= 2
+    beside = flip(far.pop(0), "row", 1, n_row)
+    pieces = {k: split(held) for k, held in far.items()}
+    pieces.update({k ^ 1: [flip(piece, "row", 1, n_row) for piece in pieces[k]] for k in far})
+    weights = [pieces[k][1] for k in range(2, n_row)]
+    (beside, weights), bundles = after((beside, weights), gather_plane(bundle))
+    bundles = with_siblings(bundles)
+
+    mixed, weight = mix([line, beside] + weights, bundles)
+    half, panel = half_of([line, beside] + [pieces[k][0] for k in range(2, n_row)], bundles)
+    halves, mixed = with_siblings(gather_plane(half)), gather_row(mixed, n_row)
     dressed, shares = dress(weight, panel, line, bundle, halves, mixed, n_row * n_plane)
     polar = finish(lax.all_to_all(shares, EVERY, 0, 0), aux)
     return polar, dressed

time: 53.5 us -> 53.1 us (level)
  waiting for transfers between devices: 14.8 us -> 14.1 us
    ppermute x20 -> x21, waiting for transfers between devices: 14.8 us -> 14.1 us  [flip(): return lax.ppermute(value, axes, [(i, i ^ mask) for i in range(count)])]
    ppermute x20 -> x21, starting transfers between devices: 20.5 us -> 20.9 us  [flip(): return lax.ppermute(value, axes, [(i, i ^ mask) for i in range(count)])]
  transfers between devices with their start and end apart: 20 -> 21, of which waited for: 10 -> 11; matrix products, arithmetic and copies ran while one was open for 0% -> 0% of each run, Pallas kernels for 0% -> 2%
where the time goes in v1:
time: 53.1 us; the launch traced here: 52.9 us
  starting transfers between devices  20.9 us (39%)
  waiting for transfers between devices  14.1 us (27%)
  blocking collectives  12.4 us (23%)
  Pallas kernels  4.23 us (8%)
  between operations  1.33 us (3%)
    ppermute x21, starting transfers between devices, flip(): return lax.ppermute(value, axes, [(i, i ^ mask) for i in range(count)])  20.9 us
    ppermute x21, waiting for transfers between devices, flip(): return lax.ppermute(value, axes, [(i, i ^ mask) for i in range(count)])  14.1 us
    all_to_all x1, blocking collectives, on_device(): polar = finish(lax.all_to_all(shares, EVERY, 0, 0), aux)  12.4 us
    pallas_call x1, Pallas kernels, dress(): pl.pallas_call(functools.partial(dress_kernel, n_row, n_plane, n_all, wei...  1.67 us
    pallas_call x1, Pallas kernels, place(): pl.pallas_call(functools.partial(place_kernel, nu // tile), out_shape=[ja...  1.07 us
  transfers between devices with their start and end apart: 21, of which 11 were waited for; matrix products, arithmetic and copies ran while one was open for 0% of the time, Pallas kernels for 2%

profile of v1, /device:TPU:0, one launch (start us, length us, event | category | flops | bytes accessed | tf_op | source)
XLA Modules:
  0.0 52.9 jit_solution(4909808772024848185)
XLA Ops:
  1.3 1.1 %place.1 = (bf16[3,128,256]{2,1,0:T(8,128)(2,1)S(1)}, bf16[3,128,256]{2,1,0:T(8,128)(2,1)S(1)}) custom-call(s32[1]{0:T(128)S(6)} %copy.7.counts_ref, s32[2]{0:T(128)} %pairs_any.1, bf16[2,4,128,128]{3,2,1,0:T(8,128)(2,1)} %tiles_any.1, bf16[128,256]{1,0:T(8,128)(2,1)} %weight_any.1, bf16[128,256]{1,0:T(8,128)(2,1)} %column_any.1), custom_call_target="tpu_custom_call" | custom-call | bytes 786432 | tf_op jit(solution)/shard_map/place/pallas_call | solution.py:99
  2.4 4.1 %collective-permute-start.1 = (bf16[3,128,256]{2,1,0:T(8,128)(2,1)S(1)}, bf16[3,128,256]{2,1,0:T(8,128)(2,1)S(1)}, u32[]{:S(2)}, u32[]{:S(2)}) collective-permute-start(bf16[3,128,256]{2,1,0:T(8,128)(2,1)S(1)} %get-tuple-element.19.refs_0_.line_ref), channel_id=1, source_target_pairs={{0,16},{8,24},{16,0},{24,8},{1,17},{9,25},{17,1},{25,9},{2,18},{10... | collective-permute-start | bytes 589832 | tf_op jit(solution)/shard_map/ppermute | solution.py:18
  6.5 1.6 %collective-permute-start = (bf16[3,128,256]{2,1,0:T(8,128)(2,1)S(1)}, bf16[3,128,256]{2,1,0:T(8,128)(2,1)S(1)}, u32[]{:S(2)}, u32[]{:S(2)}) collective-permute-start(bf16[3,128,256]{2,1,0:T(8,128)(2,1)S(1)} %get-tuple-element.19.refs_0_.line_ref), channel_id=1, source_target_pairs={{0,8},{8,0},{16,24},{24,16},{1,9},{9,1},{17,25},{25,17},{2,10},{10... | collective-permute-start | bytes 589832 | tf_op jit(solution)/shard_map/ppermute | solution.py:18
  8.0 2.4 %collective-permute-start.5 = (bf16[3,128,256]{2,1,0:T(8,128)(2,1)S(1)}, bf16[3,128,256]{2,1,0:T(8,128)(2,1)S(1)}, u32[]{:S(2)}, u32[]{:S(2)}) collective-permute-start(bf16[3,128,256]{2,1,0:T(8,128)(2,1)S(1)} %get-tuple-element.25.refs_4_.bundle_ref), channel_id=1, source_target_pairs={{0,6},{1,7},{2,4},{3,5},{4,2},{5,3},{6,0},{7,1},{8,14},{9,15},{10,... | collective-permute-start | bytes 589832 | tf_op jit(solution)/shard_map/ppermute | solution.py:18
  10.5 0.5 %collective-permute-start.4 = (bf16[3,128,256]{2,1,0:T(8,128)(2,1)S(1)}, bf16[3,128,256]{2,1,0:T(8,128)(2,1)S(1)}, u32[]{:S(2)}, u32[]{:S(2)}) collective-permute-start(bf16[3,128,256]{2,1,0:T(8,128)(2,1)S(1)} %get-tuple-element.25.refs_4_.bundle_ref), channel_id=1, source_target_pairs={{0,4},{1,5},{2,6},{3,7},{4,0},{5,1},{6,2},{7,3},{8,12},{9,13},{10,... | collective-permute-start | bytes 589832 | tf_op jit(solution)/shard_map/ppermute | solution.py:18
  11.0 0.5 collective-permute-start.3
  11.5 4.1 %collective-permute-done.1.value_ref = bf16[3,128,256]{2,1,0:T(8,128)(2,1)S(1)} collective-permute-done((bf16[3,128,256]{2,1,0:T(8,128)(2,1)S(1)}, bf16[3,128,256]{2,1,0:T(8,128)(2,1)S(1)}, u32[]{:S(2)}, u32[]{:S(2)}) %collective-permute-start.1) | collective-permute-done | bytes 196640 | tf_op jit(solution)/shard_map/ppermute | solution.py:18
  15.7 0.7 %collective-permute-start.2 = (bf16[1,128,256]{2,1,0:T(8,128)(2,1)S(1)}, bf16[1,128,256]{2,1,0:T(8,128)(2,1)S(1)}, u32[]{:S(2)}, u32[]{:S(2)}) collective-permute-start(bf16[1,128,256]{2,1,0:T(8,128)(2,1)S(1)} %get-tuple-element.23.refs_2_), channel_id=1, source_target_pairs={{0,8},{8,0},{16,24},{24,16},{1,9},{9,1},{17,25},{25,17},{2,10},{10... | collective-permute-start | bytes 196616 | tf_op jit(solution)/shard_map/ppermute | solution.py:18
  16.8 2.6 %collective-permute-done.4.refs_8_ = bf16[3,128,256]{2,1,0:T(8,128)(2,1)S(1)} collective-permute-done((bf16[3,128,256]{2,1,0:T(8,128)(2,1)S(1)}, bf16[3,128,256]{2,1,0:T(8,128)(2,1)S(1)}, u32[]{:S(2)}, u32[]{:S(2)}) %collective-permute-start.4) | collective-permute-done | bytes 196640 | tf_op jit(solution)/shard_map/ppermute | solution.py:18
  19.3 0.7 %collective-permute-done.2.refs_3_ = bf16[1,128,256]{2,1,0:T(8,128)(2,1)S(1)} collective-permute-done((bf16[1,128,256]{2,1,0:T(8,128)(2,1)S(1)}, bf16[1,128,256]{2,1,0:T(8,128)(2,1)S(1)}, u32[]{:S(2)}, u32[]{:S(2)}) %collective-permute-start.2) | collective-permute-done | bytes 65568 | tf_op jit(solution)/shard_map/ppermute | solution.py:18
  21.0 0.6 %collective-permute-start.10 = (bf16[2,128,256]{2,1,0:T(8,128)(2,1)S(1)}, bf16[2,128,256]{2,1,0:T(8,128)(2,1)S(1)}, u32[]{:S(2)}, u32[]{:S(2)}) collective-permute-start(bf16[2,128,256]{2,1,0:T(8,128)(2,1)S(1)} %get-tuple-element.30.refs_2_), channel_id=1, source_target_pairs={{0,8},{8,0},{16,24},{24,16},{1,9},{9,1},{17,25},{25,17},{2,10},{10... | collective-permute-start | bytes 393224 | tf_op jit(solution)/shard_map/ppermute | solution.py:18
  22.8 2.8 %collective-permute-start.19 = (bf16[128,512]{1,0:T(8,128)(2,1)S(1)}, bf16[128,512]{1,0:T(8,128)(2,1)S(1)}, u32[]{:S(2)}, u32[]{:S(2)}) collective-permute-start(bf16[128,512]{1,0:T(8,128)(2,1)S(1)} %get-tuple-element.33.refs_8_), channel_id=1, source_target_pairs={{0,16},{8,24},{16,0},{24,8},{1,17},{9,25},{17,1},{25,9},{2,18},{10... | collective-permute-start | bytes 393224 | tf_op jit(solution)/shard_map/ppermute | solution.py:18
  25.6 1.2 %collective-permute-start.18 = (bf16[128,512]{1,0:T(8,128)(2,1)S(1)}, bf16[128,512]{1,0:T(8,128)(2,1)S(1)}, u32[]{:S(2)}, u32[]{:S(2)}) collective-permute-start(bf16[128,512]{1,0:T(8,128)(2,1)S(1)} %get-tuple-element.33.refs_8_), channel_id=1, source_target_pairs={{0,8},{8,0},{16,24},{24,16},{1,9},{9,1},{17,25},{25,17},{2,10},{10... | collective-permute-start | bytes 393224 | tf_op jit(solution)/shard_map/ppermute | solution.py:18
  27.2 2.5 %collective-permute-start.16 = (bf16[128,512]{1,0:T(8,128)(2,1)S(1)}, bf16[128,512]{1,0:T(8,128)(2,1)S(1)}, u32[]{:S(2)}, u32[]{:S(2)}) collective-permute-start(bf16[128,512]{1,0:T(8,128)(2,1)S(1)} %get-tuple-element.32.refs_0_), channel_id=1, source_target_pairs={{0,6},{1,7},{2,4},{3,5},{4,2},{5,3},{6,0},{7,1},{8,14},{9,15},{10,... | collective-permute-start | bytes 393224 | tf_op jit(solution)/shard_map/ppermute | solution.py:18
  29.7 0.5 %collective-permute-start.14 = (bf16[128,512]{1,0:T(8,128)(2,1)S(1)}, bf16[128,512]{1,0:T(8,128)(2,1)S(1)}, u32[]{:S(2)}, u32[]{:S(2)}) collective-permute-start(bf16[128,512]{1,0:T(8,128)(2,1)S(1)} %get-tuple-element.32.refs_0_), channel_id=1, source_target_pairs={{0,4},{1,5},{2,6},{3,7},{4,0},{5,1},{6,2},{7,3},{8,12},{9,13},{10,... | collective-permute-start | bytes 393224 | tf_op jit(solution)/shard_map/ppermute | solution.py:18
  30.7 1.5 %collective-permute-done.19.refs_10_ = bf16[128,512]{1,0:T(8,128)(2,1)S(1)} collective-permute-done((bf16[128,512]{1,0:T(8,128)(2,1)S(1)}, bf16[128,512]{1,0:T(8,128)(2,1)S(1)}, u32[]{:S(2)}, u32[]{:S(2)}) %collective-permute-start.19) | collective-permute-done | bytes 131104 | tf_op jit(solution)/shard_map/ppermute | solution.py:18
  32.3 1.3 %collective-permute-start.20 = (bf16[128,512]{1,0:T(8,128)(2,1)S(1)}, bf16[128,512]{1,0:T(8,128)(2,1)S(1)}, u32[]{:S(2)}, u32[]{:S(2)}) collective-permute-start(bf16[128,512]{1,0:T(8,128)(2,1)S(1)} %collective-permute-done.19.refs_10_), channel_id=1, source_target_pairs={{0,8},{8,0},{16,24},{24,16},{1,9},{9,1},{17,25},{25,17},{2,10},{10... | collective-permute-start | bytes 393224 | tf_op jit(solution)/shard_map/ppermute | solution.py:18
  33.5 1.0 %collective-permute-done.16.refs_6_ = bf16[128,512]{1,0:T(8,128)(2,1)S(1)} collective-permute-done((bf16[128,512]{1,0:T(8,128)(2,1)S(1)}, bf16[128,512]{1,0:T(8,128)(2,1)S(1)}, u32[]{:S(2)}, u32[]{:S(2)}) %collective-permute-start.16) | collective-permute-done | bytes 131104 | tf_op jit(solution)/shard_map/ppermute | solution.py:18
  34.6 1.5 %collective-permute-done.14.refs_4_ = bf16[128,512]{1,0:T(8,128)(2,1)S(1)} collective-permute-done((bf16[128,512]{1,0:T(8,128)(2,1)S(1)}, bf16[128,512]{1,0:T(8,128)(2,1)S(1)}, u32[]{:S(2)}, u32[]{:S(2)}) %collective-permute-start.14) | collective-permute-done | bytes 131104 | tf_op jit(solution)/shard_map/ppermute | solution.py:18
  36.1 0.5 collective-permute-start.13
  36.6 1.5 %collective-permute-done.20.refs_11_ = bf16[128,512]{1,0:T(8,128)(2,1)S(1)} collective-permute-done((bf16[128,512]{1,0:T(8,128)(2,1)S(1)}, bf16[128,512]{1,0:T(8,128)(2,1)S(1)}, u32[]{:S(2)}, u32[]{:S(2)}) %collective-permute-start.20) | collective-permute-done | bytes 131104 | tf_op jit(solution)/shard_map/ppermute | solution.py:18
  38.2 1.7 %dress.1 = (bf16[128,4,256]{2,1,0:T(4,128)(2,1)}, f32[32,1,128]{2,1,0:T(1,128)S(1)}) custom-call(bf16[128,1024]{1,0:T(8,128)(2,1)S(1)} %get-tuple-element.29.weight_ref, bf16[1024,256]{1,0:T(8,128)(2,1)S(1)} %get-tuple-element.31.panel_ref, bf16[3,128,256]{2,1,0:T(8,128)(2,1)S(1)} %get-tuple-element.19.refs_0_.line_ref, ...), custom_call_target="tpu_custom_call" | custom-call | flops 268435456 | bytes 4194304 | tf_op jit(solution)/shard_map/dress/pallas_call | solution.py:223
  39.9 12.4 %all_to_all.5.shares_ref = f32[32,1,128]{2,1,0:T(1,128)S(1)} all-to-all(f32[32,1,128]{2,1,0:T(1,128)S(1)} %get-tuple-element.34), channel_id=1, replica_groups=mesh['row'=4,'col'=2,'rep'=4] {'row','col','rep'}, dimensions={0} | all-to-all | bytes 32768 | tf_op jit(solution)/shard_map/all_to_all | solution.py:285
  52.2 0.7 %finish.1 = f32[4,4]{1,0:T(4,128)} custom-call(f32[32,1,128]{2,1,0:T(1,128)S(1)} %all_to_all.5.shares_ref), custom_call_target="tpu_custom_call" | custom-call | tf_op jit(solution)/shard_map/finish/pallas_call | solution.py:247
  (25 shorter events, 3.4 us)
Async XLA Ops:
  2.4 13.3 %collective-permute-start.1 = (bf16[3,128,256]{2,1,0:T(8,128)(2,1)S(1)}, bf16[3,128,256]{2,1,0:T(8,128)(2,1)S(1)}, u32[]{:S(2)}, u32[]{:S(2)}) collective-permute-start(bf16[3,128,256]{2,1,0:T(8,128)(2,1)S(1)} %get-tuple-element.19.refs_0_.line_ref), channel_id=1, source_target_pairs={{0,16},{8,24},{16,0},{24,8},{1,17},{9,25},{17,1},{25,9},{2,18},{10... | collective-permute-start | bytes 589832 | tf_op jit(solution)/shard_map/ppermute | solution.py:18
  6.5 9.9 %collective-permute-start = (bf16[3,128,256]{2,1,0:T(8,128)(2,1)S(1)}, bf16[3,128,256]{2,1,0:T(8,128)(2,1)S(1)}, u32[]{:S(2)}, u32[]{:S(2)}) collective-permute-start(bf16[3,128,256]{2,1,0:T(8,128)(2,1)S(1)} %get-tuple-element.19.refs_0_.line_ref), channel_id=1, source_target_pairs={{0,8},{8,0},{16,24},{24,16},{1,9},{9,1},{17,25},{25,17},{2,10},{10... | collective-permute-start | bytes 589832 | tf_op jit(solution)/shard_map/ppermute | solution.py:18
  8.0 8.7 %collective-permute-start.5 = (bf16[3,128,256]{2,1,0:T(8,128)(2,1)S(1)}, bf16[3,128,256]{2,1,0:T(8,128)(2,1)S(1)}, u32[]{:S(2)}, u32[]{:S(2)}) collective-permute-start(bf16[3,128,256]{2,1,0:T(8,128)(2,1)S(1)} %get-tuple-element.25.refs_4_.bundle_ref), channel_id=1, source_target_pairs={{0,6},{1,7},{2,4},{3,5},{4,2},{5,3},{6,0},{7,1},{8,14},{9,15},{10,... | collective-permute-start | bytes 589832 | tf_op jit(solution)/shard_map/ppermute | solution.py:18
  10.5 8.8 %collective-permute-start.4 = (bf16[3,128,256]{2,1,0:T(8,128)(2,1)S(1)}, bf16[3,128,256]{2,1,0:T(8,128)(2,1)S(1)}, u32[]{:S(2)}, u32[]{:S(2)}) collective-permute-start(bf16[3,128,256]{2,1,0:T(8,128)(2,1)S(1)} %get-tuple-element.25.refs_4_.bundle_ref), channel_id=1, source_target_pairs={{0,4},{1,5},{2,6},{3,7},{4,0},{5,1},{6,2},{7,3},{8,12},{9,13},{10,... | collective-permute-start | bytes 589832 | tf_op jit(solution)/shard_map/ppermute | solution.py:18
  11.0 8.3 %collective-permute-start.3 = (bf16[3,128,256]{2,1,0:T(8,128)(2,1)S(1)}, bf16[3,128,256]{2,1,0:T(8,128)(2,1)S(1)}, u32[]{:S(2)}, u32[]{:S(2)}) collective-permute-start(bf16[3,128,256]{2,1,0:T(8,128)(2,1)S(1)} %get-tuple-element.25.refs_4_.bundle_ref), channel_id=1, source_target_pairs={{0,2},{1,3},{2,0},{3,1},{4,6},{5,7},{6,4},{7,5},{8,10},{9,11},{10,... | collective-permute-start | bytes 589832 | tf_op jit(solution)/shard_map/ppermute | solution.py:18
  15.7 4.3 %collective-permute-start.2 = (bf16[1,128,256]{2,1,0:T(8,128)(2,1)S(1)}, bf16[1,128,256]{2,1,0:T(8,128)(2,1)S(1)}, u32[]{:S(2)}, u32[]{:S(2)}) collective-permute-start(bf16[1,128,256]{2,1,0:T(8,128)(2,1)S(1)} %get-tuple-element.23.refs_2_), channel_id=1, source_target_pairs={{0,8},{8,0},{16,24},{24,16},{1,9},{9,1},{17,25},{25,17},{2,10},{10... | collective-permute-start | bytes 196616 | tf_op jit(solution)/shard_map/ppermute | solution.py:18
  20.0 1.6 %collective-permute-start.6 = (bf16[3,128,256]{2,1,0:T(8,128)(2,1)S(1)}, bf16[3,128,256]{2,1,0:T(8,128)(2,1)S(1)}, u32[]{:S(2)}, u32[]{:S(2)}) collective-permute-start(bf16[3,128,256]{2,1,0:T(8,128)(2,1)S(1)} %get-tuple-element.25.refs_4_.bundle_ref), channel_id=1, source_target_pairs={{0,1},{1,0},{2,3},{3,2},{4,5},{5,4},{6,7},{7,6},{8,9},{9,8},{10,11... | collective-permute-start | bytes 589832 | tf_op jit(solution)/shard_map/ppermute | solution.py:18
  20.0 1.7 %collective-permute-start.7 = (bf16[3,128,256]{2,1,0:T(8,128)(2,1)S(1)}, bf16[3,128,256]{2,1,0:T(8,128)(2,1)S(1)}, u32[]{:S(2)}, u32[]{:S(2)}) collective-permute-start(bf16[3,128,256]{2,1,0:T(8,128)(2,1)S(1)} %collective-permute-done.3.refs_6_), channel_id=1, source_target_pairs={{0,1},{1,0},{2,3},{3,2},{4,5},{5,4},{6,7},{7,6},{8,9},{9,8},{10,11... | collective-permute-start | bytes 589832 | tf_op jit(solution)/shard_map/ppermute | solution.py:18
  20.5 1.5 %collective-permute-start.8 = (bf16[3,128,256]{2,1,0:T(8,128)(2,1)S(1)}, bf16[3,128,256]{2,1,0:T(8,128)(2,1)S(1)}, u32[]{:S(2)}, u32[]{:S(2)}) collective-permute-start(bf16[3,128,256]{2,1,0:T(8,128)(2,1)S(1)} %collective-permute-done.4.refs_8_), channel_id=1, source_target_pairs={{0,1},{1,0},{2,3},{3,2},{4,5},{5,4},{6,7},{7,6},{8,9},{9,8},{10,11... | collective-permute-start | bytes 589832 | tf_op jit(solution)/shard_map/ppermute | solution.py:18
  20.5 1.8 %collective-permute-start.9 = (bf16[3,128,256]{2,1,0:T(8,128)(2,1)S(1)}, bf16[3,128,256]{2,1,0:T(8,128)(2,1)S(1)}, u32[]{:S(2)}, u32[]{:S(2)}) collective-permute-start(bf16[3,128,256]{2,1,0:T(8,128)(2,1)S(1)} %collective-permute-done.5.refs_10_), channel_id=1, source_target_pairs={{0,1},{1,0},{2,3},{3,2},{4,5},{5,4},{6,7},{7,6},{8,9},{9,8},{10,11... | collective-permute-start | bytes 589832 | tf_op jit(solution)/shard_map/ppermute | solution.py:18
  21.0 5.8 %collective-permute-start.10 = (bf16[2,128,256]{2,1,0:T(8,128)(2,1)S(1)}, bf16[2,128,256]{2,1,0:T(8,128)(2,1)S(1)}, u32[]{:S(2)}, u32[]{:S(2)}) collective-permute-start(bf16[2,128,256]{2,1,0:T(8,128)(2,1)S(1)} %get-tuple-element.30.refs_2_), channel_id=1, source_target_pairs={{0,8},{8,0},{16,24},{24,16},{1,9},{9,1},{17,25},{25,17},{2,10},{10... | collective-permute-start | bytes 393224 | tf_op jit(solution)/shard_map/ppermute | solution.py:18
  22.8 9.5 %collective-permute-start.19 = (bf16[128,512]{1,0:T(8,128)(2,1)S(1)}, bf16[128,512]{1,0:T(8,128)(2,1)S(1)}, u32[]{:S(2)}, u32[]{:S(2)}) collective-permute-start(bf16[128,512]{1,0:T(8,128)(2,1)S(1)} %get-tuple-element.33.refs_8_), channel_id=1, source_target_pairs={{0,16},{8,24},{16,0},{24,8},{1,17},{9,25},{17,1},{25,9},{2,18},{10... | collective-permute-start | bytes 393224 | tf_op jit(solution)/shard_map/ppermute | solution.py:18
  25.6 6.7 %collective-permute-start.18 = (bf16[128,512]{1,0:T(8,128)(2,1)S(1)}, bf16[128,512]{1,0:T(8,128)(2,1)S(1)}, u32[]{:S(2)}, u32[]{:S(2)}) collective-permute-start(bf16[128,512]{1,0:T(8,128)(2,1)S(1)} %get-tuple-element.33.refs_8_), channel_id=1, source_target_pairs={{0,8},{8,0},{16,24},{24,16},{1,9},{9,1},{17,25},{25,17},{2,10},{10... | collective-permute-start | bytes 393224 | tf_op jit(solution)/shard_map/ppermute | solution.py:18
  27.2 7.4 %collective-permute-start.16 = (bf16[128,512]{1,0:T(8,128)(2,1)S(1)}, bf16[128,512]{1,0:T(8,128)(2,1)S(1)}, u32[]{:S(2)}, u32[]{:S(2)}) collective-permute-start(bf16[128,512]{1,0:T(8,128)(2,1)S(1)} %get-tuple-element.32.refs_0_), channel_id=1, source_target_pairs={{0,6},{1,7},{2,4},{3,5},{4,2},{5,3},{6,0},{7,1},{8,14},{9,15},{10,... | collective-permute-start | bytes 393224 | tf_op jit(solution)/shard_map/ppermute | solution.py:18
  29.7 6.4 %collective-permute-start.14 = (bf16[128,512]{1,0:T(8,128)(2,1)S(1)}, bf16[128,512]{1,0:T(8,128)(2,1)S(1)}, u32[]{:S(2)}, u32[]{:S(2)}) collective-permute-start(bf16[128,512]{1,0:T(8,128)(2,1)S(1)} %get-tuple-element.32.refs_0_), channel_id=1, source_target_pairs={{0,4},{1,5},{2,6},{3,7},{4,0},{5,1},{6,2},{7,3},{8,12},{9,13},{10,... | collective-permute-start | bytes 393224 | tf_op jit(solution)/shard_map/ppermute | solution.py:18
  30.2 5.9 %collective-permute-start.12 = (bf16[128,512]{1,0:T(8,128)(2,1)S(1)}, bf16[128,512]{1,0:T(8,128)(2,1)S(1)}, u32[]{:S(2)}, u32[]{:S(2)}) collective-permute-start(bf16[128,512]{1,0:T(8,128)(2,1)S(1)} %get-tuple-element.32.refs_0_), channel_id=1, source_target_pairs={{0,2},{1,3},{2,0},{3,1},{4,6},{5,7},{6,4},{7,5},{8,10},{9,11},{10,... | collective-permute-start | bytes 393224 | tf_op jit(solution)/shard_map/ppermute | solution.py:18
  32.3 4.4 %collective-permute-start.11 = (bf16[128,512]{1,0:T(8,128)(2,1)S(1)}, bf16[128,512]{1,0:T(8,128)(2,1)S(1)}, u32[]{:S(2)}, u32[]{:S(2)}) collective-permute-start(bf16[128,512]{1,0:T(8,128)(2,1)S(1)} %get-tuple-element.32.refs_0_), channel_id=1, source_target_pairs={{0,1},{1,0},{2,3},{3,2},{4,5},{5,4},{6,7},{7,6},{8,9},{9,8},{10,11... | collective-permute-start | bytes 393224 | tf_op jit(solution)/shard_map/ppermute | solution.py:18
  32.3 5.9 %collective-permute-start.20 = (bf16[128,512]{1,0:T(8,128)(2,1)S(1)}, bf16[128,512]{1,0:T(8,128)(2,1)S(1)}, u32[]{:S(2)}, u32[]{:S(2)}) collective-permute-start(bf16[128,512]{1,0:T(8,128)(2,1)S(1)} %collective-permute-done.19.refs_10_), channel_id=1, source_target_pairs={{0,8},{8,0},{16,24},{24,16},{1,9},{9,1},{17,25},{25,17},{2,10},{10... | collective-permute-start | bytes 393224 | tf_op jit(solution)/shard_map/ppermute | solution.py:18
  34.6 3.6 %collective-permute-start.17 = (bf16[128,512]{1,0:T(8,128)(2,1)S(1)}, bf16[128,512]{1,0:T(8,128)(2,1)S(1)}, u32[]{:S(2)}, u32[]{:S(2)}) collective-permute-start(bf16[128,512]{1,0:T(8,128)(2,1)S(1)} %collective-permute-done.16.refs_6_), channel_id=1, source_target_pairs={{0,1},{1,0},{2,3},{3,2},{4,5},{5,4},{6,7},{7,6},{8,9},{9,8},{10,11... | collective-permute-start | bytes 393224 | tf_op jit(solution)/shard_map/ppermute | solution.py:18
  36.1 2.1 %collective-permute-start.15 = (bf16[128,512]{1,0:T(8,128)(2,1)S(1)}, bf16[128,512]{1,0:T(8,128)(2,1)S(1)}, u32[]{:S(2)}, u32[]{:S(2)}) collective-permute-start(bf16[128,512]{1,0:T(8,128)(2,1)S(1)} %collective-permute-done.14.refs_4_), channel_id=1, source_target_pairs={{0,1},{1,0},{2,3},{3,2},{4,5},{5,4},{6,7},{7,6},{8,9},{9,8},{10,11... | collective-permute-start | bytes 393224 | tf_op jit(solution)/shard_map/ppermute | solution.py:18
  36.1 2.1 %collective-permute-start.13 = (bf16[128,512]{1,0:T(8,128)(2,1)S(1)}, bf16[128,512]{1,0:T(8,128)(2,1)S(1)}, u32[]{:S(2)}, u32[]{:S(2)}) collective-permute-start(bf16[128,512]{1,0:T(8,128)(2,1)S(1)} %collective-permute-done.12.refs_2_), channel_id=1, source_target_pairs={{0,1},{1,0},{2,3},{3,2},{4,5},{5,4},{6,7},{7,6},{8,9},{9,8},{10,11... | collective-permute-start | bytes 393224 | tf_op jit(solution)/shard_map/ppermute | solution.py:18
